TPU v7x, 32 devices: a whole 2x2x4 slice. The times are simulated.
32 devices in a mesh: section: 4 (over y, core), node: 8 (over z, x).
Axes of the slice: x: 2, y: 2, z: 4, core: 2. Of those that a mesh axis runs over, the one named last changes fastest.
Arguments:
- acts: bfloat16 [4, 3, 2048, 512], P('section', None, 'node'), may hold values from -6 to 6
- top_grad: bfloat16 [3, 2048, 512], P(None, 'node'), may hold values from -6 to 6
- w_in: bfloat16 [4, 512, 1024], P('section'), may hold values from -0.25 to 0.25
- w_out: bfloat16 [4, 1024, 512], P('section'), may hold values from -0.1875 to 0.1875
- tile_table: bfloat16 [3, 64, 128, 128], P(None, 'node'), may hold values from -0.25 to 0.25
- tile_rows: int32 [3, 64], P(None, 'node'), may hold values from 0 to 1
- tile_cols: int32 [3, 64], P(None, 'node'), may hold values from 0 to 15, as said below
- tile_ids: int32 [3, 64], P(None, 'node'), may hold values from 0 to 7
- tile_count: int32 [3, 8], P(None, 'node'), may hold values from 4 to 8, as said below
Outputs:
- act_grads: bfloat16 [4, 3, 2048, 512], P('section', None, 'node')
- w_in_grad: float32 [4, 512, 1024], P('section')
- w_out_grad: float32 [4, 1024, 512], P('section')
Inputs may be any that keep to these rules, and one draw needn't show every extreme that they name: `tile_cols`: A tile slot's column block lies on its own device or on the next or previous device along node, wrapping around; of one device's 8 slots at most 2 have columns on the next device and at most 2 on the previous one, and in every group some device has exactly 2 live slots with columns on the next device. Slots k < tile_count of a device are live; in every group some device has 8.
All inputs are finite; a program needn't handle non-finite values.
Results may differ from a plain program's by a relative error of at most 0.03.
Values may be sent and summed in bfloat16 or wider, within the bound.
A program may use at most 64 MiB of HBM per device.

v0:
```python
import jax
import jax.numpy as jnp
from jax import lax
from jax.sharding import PartitionSpec as P


def shifted(block, axis, distance):
    devices = range(lax.axis_size(axis))
    route = [(i - distance, i) for i in devices if i - distance in devices]
    return lax.ppermute(block, axis, route)


def passed_along(block, axis, distance):
    devices = range(lax.axis_size(axis))
    route = [((i - distance) % len(devices), i) for i in devices]
    return lax.ppermute(block, axis, route)


def shards(acts, top_grad, w_in, w_out, tile_table, tile_rows, tile_cols, tile_ids, tile_count):
    sections = lax.axis_size("section")
    node_count = lax.axis_size("node")
    section_idx = lax.axis_index("section")
    node_idx = lax.axis_index("node")
    groups, row_count, feature_dim = top_grad.shape
    block_size = tile_table.shape[-1]
    block_count = row_count // block_size
    hidden_dim = w_in.shape[2]
    slot_total = tile_rows.shape[1]
    layer_inputs = acts[0]
    w_first = w_in[0]
    w_second = w_out[0]
    block_range = jnp.arange(block_count, dtype=jnp.int32)
    slot_range = jnp.arange(slot_total, dtype=jnp.int32)

    def mlp_back(operands):
        layer_in, grad_now, grad_mid = operands
        pre = jnp.dot(layer_in, w_first, preferred_element_type=jnp.float32)
        sigma = jax.nn.sigmoid(pre)
        act_val = (pre * sigma).astype(jnp.bfloat16)
        second_inc = lax.dot_general(
            act_val, grad_mid, (((0,), (0,)), ((), ())), preferred_element_type=jnp.float32
        )
        dact = lax.dot_general(
            grad_mid, w_second, (((1,), (1,)), ((), ())), preferred_element_type=jnp.float32
        )
        dpre = (dact * sigma * (1.0 + pre * (1.0 - sigma))).astype(jnp.bfloat16)
        first_inc = lax.dot_general(
            layer_in, dpre, (((0,), (0,)), ((), ())), preferred_element_type=jnp.float32
        )
        back = lax.dot_general(
            dpre, w_first, (((1,), (1,)), ((), ())), preferred_element_type=jnp.float32
        )
        new_grad = (grad_now.astype(jnp.float32) + back).astype(jnp.bfloat16)
        return (new_grad, first_inc, second_inc)

    def mlp_skip(operands):
        return (
            jnp.zeros((row_count, feature_dim), jnp.bfloat16),
            jnp.zeros((feature_dim, hidden_dim), jnp.float32),
            jnp.zeros((hidden_dim, feature_dim), jnp.float32),
        )

    def advance(time_step, state_now):
        previous, grads_out, first_sum, second_sum = state_now
        group_idx = time_step - (sections - 1 - section_idx)
        active = (group_idx >= 0) & (group_idx < groups)
        group_safe = jnp.clip(group_idx, 0, groups - 1)
        incoming = shifted(previous, "section", -1)
        top_now = lax.dynamic_index_in_dim(top_grad, group_safe, 0, keepdims=False)
        grad_now = jnp.where(section_idx == sections - 1, top_now, incoming)
        row_pick = lax.dynamic_index_in_dim(tile_rows, group_safe, 0, keepdims=False)
        col_pick = lax.dynamic_index_in_dim(tile_cols, group_safe, 0, keepdims=False)
        id_pick = lax.dynamic_index_in_dim(tile_ids, group_safe, 0, keepdims=False)
        live_count = lax.dynamic_index_in_dim(tile_count, group_safe, 0, keepdims=False)[0]
        table_now = lax.dynamic_index_in_dim(tile_table, group_safe, 0, keepdims=False)
        dest_dev = col_pick // block_count
        col_local = col_pick % block_count
        offset = (dest_dev - node_idx) % node_count
        live_mask = slot_range < live_count
        tile_block = table_now[id_pick]
        pieces = grad_now.reshape(block_count, block_size, feature_dim)[row_pick]
        terms = jnp.einsum(
            "kij,kid->kjd", tile_block, pieces, preferred_element_type=jnp.float32
        ).astype(jnp.bfloat16)
        place_mask = col_local[:, None] == block_range[None, :]

        def picker(selector):
            return (place_mask & (selector & live_mask)[:, None]).astype(jnp.bfloat16)

        local_sum = jnp.einsum(
            "kb,kjd->bjd", picker(offset == 0), terms, preferred_element_type=jnp.float32
        )
        forward_mask = offset == 1
        backward_mask = offset == node_count - 1
        to_next = jnp.einsum(
            "kb,kjd->bjd", picker(forward_mask), terms, preferred_element_type=jnp.float32
        )
        to_prev = jnp.einsum(
            "kb,kjd->bjd", picker(backward_mask), terms, preferred_element_type=jnp.float32
        )
        from_prev = passed_along(to_next.astype(jnp.bfloat16), "node", 1).astype(to_next.dtype)
        from_next = passed_along(to_prev.astype(jnp.bfloat16), "node", -1).astype(to_prev.dtype)
        summed = local_sum + from_prev + from_next
        grad_mid = summed.astype(jnp.bfloat16).reshape(row_count, feature_dim)
        layer_in = lax.dynamic_index_in_dim(layer_inputs, group_safe, 0, keepdims=False)
        new_grad, first_inc, second_inc = lax.cond(
            active, mlp_back, mlp_skip, (layer_in, grad_now, grad_mid)
        )
        stored = lax.dynamic_index_in_dim(grads_out, group_safe, 0, keepdims=False)
        grads_out = lax.dynamic_update_index_in_dim(
            grads_out, jnp.where(active, new_grad, stored), group_safe, 0
        )
        return (new_grad, grads_out, first_sum + first_inc, second_sum + second_inc)

    start_state = (
        jnp.zeros((row_count, feature_dim), jnp.bfloat16),
        jnp.zeros((groups, row_count, feature_dim), jnp.bfloat16),
        jnp.zeros((feature_dim, hidden_dim), jnp.float32),
        jnp.zeros((hidden_dim, feature_dim), jnp.float32),
    )
    final_state = lax.fori_loop(0, groups + sections - 1, advance, start_state)
    first_total, second_total = (
        lax.psum(final_state[2].astype(jnp.bfloat16), "node").astype(jnp.float32),
        lax.psum(final_state[3].astype(jnp.bfloat16), "node").astype(jnp.float32),
    )
    return (final_state[1][None], first_total[None], second_total[None])


def solution(mesh):
    return jax.shard_map(
        shards,
        mesh=mesh,
        in_specs=(
            P("section", None, "node", None),
            P(None, "node", None),
            P("section", None, None),
            P("section", None, None),
            P(None, "node", None, None),
            P(None, "node"),
            P(None, "node"),
            P(None, "node"),
            P(None, "node"),
        ),
        out_specs=(
            P("section", None, "node", None),
            P("section", None, None),
            P("section", None, None),
        ),
        check_vma=False,
    )
```

profile of v0, /device:TPU:0, one launch (start us, length us, event | category | flops | bytes accessed | tf_op | source)
XLA Modules:
  0.0 355.9 jit_solution(11604861141324954208)
XLA Ops:
  8.2 223.1 %while.23 = (s32[]{:T(128)}, bf16[256,512]{1,0:T(8,128)(2,1)S(1)}, bf16[3,256,512]{2,1,0:T(8,128)(2,1)}, f32[512,1024]{1,0:T(8,128)}, f32[1024,512]{1,0:T(8,128)...) while((s32[]{:T(128)}, bf16[256,512]{1,0:T(8,128)(2,1)S(1)}, ...), condition=%wide.region_3.4_spmd.clone, body=%wide.region_0.3_spmd.clone.sunk | while | flops 1490553344 | bytes 70265608 | solution.py:121
  17.8 3.0 collective-permute-start.2
  21.5 3.1 collective-permute-start.1
  26.4 6.5 %collective-permute-done.2 = bf16[2,128,512]{2,0,1:T(2,128)(2,1)S(1)} collective-permute-done((bf16[2,128,512]{2,0,1:T(2,128)(2,1)S(1)}, bf16[2,128,512]{2,0,1:T(2,128)(2,1)S(1)}, u32[]{:S(2)}, u32[]{:S(2)}) %collective-permute-start.2) | collective-permute-done | bytes 262176 | tf_op jit(solution)/shard_map/while/body/eval_jaxpr/ppermute | solution.py:16
  32.9 3.3 collective-permute-done.1
  56.0 4.8 %collective-permute-start.1 = (bf16[2,128,512]{2,0,1:T(2,128)(2,1)S(1)}, bf16[2,128,512]{2,0,1:T(2,128)(2,1)S(1)}, u32[]{:S(2)}, u32[]{:S(2)}) collective-permute-start(bf16[2,128,512]{2,0,1:T(2,128)(2,1)S(1)} %convolution_convert_fusion.7), channel_id=1, source_target_pairs={{1,0},{2,1},{3,2},{4,3},{5,4},{6,5},{7,6},{0,7},{9,8},{10,9},{11,1... | collective-permute-start | bytes 786440 | tf_op jit(solution)/shard_map/while/body/eval_jaxpr/ppermute | solution.py:16
  62.5 4.7 %collective-permute-done.2 = bf16[2,128,512]{2,0,1:T(2,128)(2,1)S(1)} collective-permute-done((bf16[2,128,512]{2,0,1:T(2,128)(2,1)S(1)}, bf16[2,128,512]{2,0,1:T(2,128)(2,1)S(1)}, u32[]{:S(2)}, u32[]{:S(2)}) %collective-permute-start.2) | collective-permute-done | bytes 262176 | tf_op jit(solution)/shard_map/while/body/eval_jaxpr/ppermute | solution.py:16
  67.2 3.5 collective-permute-done.1
  74.2 3.5 select_add_fusion.4
  91.9 4.8 %collective-permute-start.1 = (bf16[2,128,512]{2,0,1:T(2,128)(2,1)S(1)}, bf16[2,128,512]{2,0,1:T(2,128)(2,1)S(1)}, u32[]{:S(2)}, u32[]{:S(2)}) collective-permute-start(bf16[2,128,512]{2,0,1:T(2,128)(2,1)S(1)} %convolution_convert_fusion.7), channel_id=1, source_target_pairs={{1,0},{2,1},{3,2},{4,3},{5,4},{6,5},{7,6},{0,7},{9,8},{10,9},{11,1... | collective-permute-start | bytes 786440 | tf_op jit(solution)/shard_map/while/body/eval_jaxpr/ppermute | solution.py:16
  100.4 4.3 %collective-permute-done.1 = bf16[2,128,512]{2,0,1:T(2,128)(2,1)S(1)} collective-permute-done((bf16[2,128,512]{2,0,1:T(2,128)(2,1)S(1)}, bf16[2,128,512]{2,0,1:T(2,128)(2,1)S(1)}, u32[]{:S(2)}, u32[]{:S(2)}) %collective-permute-start.1) | collective-permute-done | bytes 262176 | tf_op jit(solution)/shard_map/while/body/eval_jaxpr/ppermute | solution.py:16
  108.2 3.5 select_add_fusion.4
  127.8 4.8 %collective-permute-start.1 = (bf16[2,128,512]{2,0,1:T(2,128)(2,1)S(1)}, bf16[2,128,512]{2,0,1:T(2,128)(2,1)S(1)}, u32[]{:S(2)}, u32[]{:S(2)}) collective-permute-start(bf16[2,128,512]{2,0,1:T(2,128)(2,1)S(1)} %convolution_convert_fusion.7), channel_id=1, source_target_pairs={{1,0},{2,1},{3,2},{4,3},{5,4},{6,5},{7,6},{0,7},{9,8},{10,9},{11,1... | collective-permute-start | bytes 786440 | tf_op jit(solution)/shard_map/while/body/eval_jaxpr/ppermute | solution.py:16
  138.0 5.8 %conditional.3 = (bf16[256,512]{1,0:T(8,128)(2,1)S(1)}, f32[512,1024]{1,0:T(8,128)S(1)}, f32[1024,512]{1,0:T(8,128)}) conditional(s32[]{:T(128)} %convert_element_type.145, () %tuple.74, (bf16[256,512]{1,0:T(8,128)(2,1)S(1)}, bf16[2,128,512]{2,0,1:T(2,128)(2,1)S(1)}, bf16[1024,512]{1,0:T(8,128)(2,1)S(1)}, bf16[3,256,512]{2,1,0:T(8,128)(2,1)}, ...), branch_computations={%region_1.1_spmd, %region_2.2_spmd} | conditional | flops 1346240512 | bytes 14156824 | solution.py:106
  144.5 3.5 select_add_fusion.4
  158.5 5.0 %collective-permute-done = bf16[256,512]{1,0:T(8,128)(2,1)S(1)} collective-permute-done((bf16[256,512]{1,0:T(8,128)(2,1)S(1)}, bf16[256,512]{1,0:T(8,128)(2,1)S(1)}, u32[]{:S(2)}, u32[]{:S(2)}) %collective-permute-start) | collective-permute-done | bytes 262176 | tf_op jit(solution)/shard_map/while/body/eval_jaxpr/ppermute | solution.py:10
  167.1 4.8 %collective-permute-start.1 = (bf16[2,128,512]{2,0,1:T(2,128)(2,1)S(1)}, bf16[2,128,512]{2,0,1:T(2,128)(2,1)S(1)}, u32[]{:S(2)}, u32[]{:S(2)}) collective-permute-start(bf16[2,128,512]{2,0,1:T(2,128)(2,1)S(1)} %convolution_convert_fusion.7), channel_id=1, source_target_pairs={{1,0},{2,1},{3,2},{4,3},{5,4},{6,5},{7,6},{0,7},{9,8},{10,9},{11,1... | collective-permute-start | bytes 786440 | tf_op jit(solution)/shard_map/while/body/eval_jaxpr/ppermute | solution.py:16
  177.4 5.8 %conditional.3 = (bf16[256,512]{1,0:T(8,128)(2,1)S(1)}, f32[512,1024]{1,0:T(8,128)S(1)}, f32[1024,512]{1,0:T(8,128)}) conditional(s32[]{:T(128)} %convert_element_type.145, () %tuple.74, (bf16[256,512]{1,0:T(8,128)(2,1)S(1)}, bf16[2,128,512]{2,0,1:T(2,128)(2,1)S(1)}, bf16[1024,512]{1,0:T(8,128)(2,1)S(1)}, bf16[3,256,512]{2,1,0:T(8,128)(2,1)}, ...), branch_computations={%region_1.1_spmd, %region_2.2_spmd} | conditional | flops 1346240512 | bytes 14156824 | solution.py:106
  183.9 3.5 select_add_fusion.4
  197.8 5.8 %collective-permute-done = bf16[256,512]{1,0:T(8,128)(2,1)S(1)} collective-permute-done((bf16[256,512]{1,0:T(8,128)(2,1)S(1)}, bf16[256,512]{1,0:T(8,128)(2,1)S(1)}, u32[]{:S(2)}, u32[]{:S(2)}) %collective-permute-start) | collective-permute-done | bytes 262176 | tf_op jit(solution)/shard_map/while/body/eval_jaxpr/ppermute | solution.py:10
  207.3 4.8 %collective-permute-start.1 = (bf16[2,128,512]{2,0,1:T(2,128)(2,1)S(1)}, bf16[2,128,512]{2,0,1:T(2,128)(2,1)S(1)}, u32[]{:S(2)}, u32[]{:S(2)}) collective-permute-start(bf16[2,128,512]{2,0,1:T(2,128)(2,1)S(1)} %convolution_convert_fusion.7), channel_id=1, source_target_pairs={{1,0},{2,1},{3,2},{4,3},{5,4},{6,5},{7,6},{0,7},{9,8},{10,9},{11,1... | collective-permute-start | bytes 786440 | tf_op jit(solution)/shard_map/while/body/eval_jaxpr/ppermute | solution.py:16
  217.5 5.8 %conditional.3 = (bf16[256,512]{1,0:T(8,128)(2,1)S(1)}, f32[512,1024]{1,0:T(8,128)S(1)}, f32[1024,512]{1,0:T(8,128)}) conditional(s32[]{:T(128)} %convert_element_type.145, () %tuple.74, (bf16[256,512]{1,0:T(8,128)(2,1)S(1)}, bf16[2,128,512]{2,0,1:T(2,128)(2,1)S(1)}, bf16[1024,512]{1,0:T(8,128)(2,1)S(1)}, bf16[3,256,512]{2,1,0:T(8,128)(2,1)}, ...), branch_computations={%region_1.1_spmd, %region_2.2_spmd} | conditional | flops 1346240512 | bytes 14156824 | solution.py:106
  224.0 3.5 select_add_fusion.4
  235.3 109.2 %all-reduce.3.cloned.1.call-done = (bf16[1,512,1024]{2,1,0:T(8,128)(2,1)}, bf16[1,1024,512]{2,1,0:T(8,128)(2,1)}) async-done(((bf16[1,512,1024]{2,1,0:T(8,128)(2,1)}, bf16[1,1024,512]{2,1,0:T(8,128)(2,1)}), (bf16[1,512,1024]{2,1,0:T(8,128)(2,1)}, bf16[1,1024,512]{2,1,0:T(8,128)(2,1)})) %all-reduce.3.cloned.1.call-update) | async-done | bytes 2097168 | tf_op jit(solution)/shard_map/psum | solution.py:123
  (259 shorter events, 156.6 us)
Async XLA Ops:
  7.2 337.4 %all-reduce.3.cloned.1.call-start = ((), (), s32[]{:S(2)}) async-start(), calls=%async_computation | async-start | bytes 4194304 | tf_op jit(solution)/shard_map/psum | solution.py:123
  8.2 6.7 %collective-permute-start = (bf16[256,512]{1,0:T(8,128)(2,1)S(1)}, bf16[256,512]{1,0:T(8,128)(2,1)S(1)}, u32[]{:S(2)}, u32[]{:S(2)}) collective-permute-start(bf16[256,512]{1,0:T(8,128)(2,1)S(1)} %get-tuple-element.801), channel_id=1, source_target_pairs={{8,0},{16,8},{24,16},{9,1},{17,9},{25,17},{10,2},{18,10},{26,18},{... | collective-permute-start | bytes 786440 | tf_op jit(solution)/shard_map/while/body/eval_jaxpr/ppermute | solution.py:10
  17.8 15.2 %collective-permute-start.2 = (bf16[2,128,512]{2,0,1:T(2,128)(2,1)S(1)}, bf16[2,128,512]{2,0,1:T(2,128)(2,1)S(1)}, u32[]{:S(2)}, u32[]{:S(2)}) collective-permute-start(bf16[2,128,512]{2,0,1:T(2,128)(2,1)S(1)} %convolution_convert_fusion.8), channel_id=1, source_target_pairs={{7,0},{0,1},{1,2},{2,3},{3,4},{4,5},{5,6},{6,7},{15,8},{8,9},{9,10... | collective-permute-start | bytes 786440 | tf_op jit(solution)/shard_map/while/body/eval_jaxpr/ppermute | solution.py:16
  21.5 15.6 %copy-start = (bf16[512,1024]{1,0:T(8,128)(2,1)S(1)}, bf16[512,1024]{1,0:T(8,128)(2,1)}, u32[]{:S(2)}) copy-start(bf16[512,1024]{1,0:T(8,128)(2,1)} %get-tuple-element.837) | copy-start | bytes 3145732 | tf_op jit(solution)/shard_map/while
  21.5 14.7 %collective-permute-start.1 = (bf16[2,128,512]{2,0,1:T(2,128)(2,1)S(1)}, bf16[2,128,512]{2,0,1:T(2,128)(2,1)S(1)}, u32[]{:S(2)}, u32[]{:S(2)}) collective-permute-start(bf16[2,128,512]{2,0,1:T(2,128)(2,1)S(1)} %convolution_convert_fusion.7), channel_id=1, source_target_pairs={{1,0},{2,1},{3,2},{4,3},{5,4},{6,5},{7,6},{0,7},{9,8},{10,9},{11,1... | collective-permute-start | bytes 786440 | tf_op jit(solution)/shard_map/while/body/eval_jaxpr/ppermute | solution.py:16
  24.6 12.5 %copy-start.8 = (bf16[1024,512]{1,0:T(8,128)(2,1)S(1)}, bf16[1024,512]{1,0:T(8,128)(2,1)}, u32[]{:S(2)}) copy-start(bf16[1024,512]{1,0:T(8,128)(2,1)} %get-tuple-element.835) | copy-start | bytes 3145732 | tf_op jit(solution)/shard_map/while
  45.6 6.7 %collective-permute-start = (bf16[256,512]{1,0:T(8,128)(2,1)S(1)}, bf16[256,512]{1,0:T(8,128)(2,1)S(1)}, u32[]{:S(2)}, u32[]{:S(2)}) collective-permute-start(bf16[256,512]{1,0:T(8,128)(2,1)S(1)} %get-tuple-element.801), channel_id=1, source_target_pairs={{8,0},{16,8},{24,16},{9,1},{17,9},{25,17},{10,2},{18,10},{26,18},{... | collective-permute-start | bytes 786440 | tf_op jit(solution)/shard_map/while/body/eval_jaxpr/ppermute | solution.py:10
  55.2 12.0 %collective-permute-start.2 = (bf16[2,128,512]{2,0,1:T(2,128)(2,1)S(1)}, bf16[2,128,512]{2,0,1:T(2,128)(2,1)S(1)}, u32[]{:S(2)}, u32[]{:S(2)}) collective-permute-start(bf16[2,128,512]{2,0,1:T(2,128)(2,1)S(1)} %convolution_convert_fusion.8), channel_id=1, source_target_pairs={{7,0},{0,1},{1,2},{2,3},{3,4},{4,5},{5,6},{6,7},{15,8},{8,9},{9,10... | collective-permute-start | bytes 786440 | tf_op jit(solution)/shard_map/while/body/eval_jaxpr/ppermute | solution.py:16
  56.0 15.6 %copy-start = (bf16[512,1024]{1,0:T(8,128)(2,1)S(1)}, bf16[512,1024]{1,0:T(8,128)(2,1)}, u32[]{:S(2)}) copy-start(bf16[512,1024]{1,0:T(8,128)(2,1)} %get-tuple-element.837) | copy-start | bytes 3145732 | tf_op jit(solution)/shard_map/while
  56.0 14.7 %collective-permute-start.1 = (bf16[2,128,512]{2,0,1:T(2,128)(2,1)S(1)}, bf16[2,128,512]{2,0,1:T(2,128)(2,1)S(1)}, u32[]{:S(2)}, u32[]{:S(2)}) collective-permute-start(bf16[2,128,512]{2,0,1:T(2,128)(2,1)S(1)} %convolution_convert_fusion.7), channel_id=1, source_target_pairs={{1,0},{2,1},{3,2},{4,3},{5,4},{6,5},{7,6},{0,7},{9,8},{10,9},{11,1... | collective-permute-start | bytes 786440 | tf_op jit(solution)/shard_map/while/body/eval_jaxpr/ppermute | solution.py:16
  60.8 10.8 %copy-start.8 = (bf16[1024,512]{1,0:T(8,128)(2,1)S(1)}, bf16[1024,512]{1,0:T(8,128)(2,1)}, u32[]{:S(2)}) copy-start(bf16[1024,512]{1,0:T(8,128)(2,1)} %get-tuple-element.835) | copy-start | bytes 3145732 | tf_op jit(solution)/shard_map/while
  81.5 6.7 %collective-permute-start = (bf16[256,512]{1,0:T(8,128)(2,1)S(1)}, bf16[256,512]{1,0:T(8,128)(2,1)S(1)}, u32[]{:S(2)}, u32[]{:S(2)}) collective-permute-start(bf16[256,512]{1,0:T(8,128)(2,1)S(1)} %get-tuple-element.801), channel_id=1, source_target_pairs={{8,0},{16,8},{24,16},{9,1},{17,9},{25,17},{10,2},{18,10},{26,18},{... | collective-permute-start | bytes 786440 | tf_op jit(solution)/shard_map/while/body/eval_jaxpr/ppermute | solution.py:10
  91.0 9.3 %collective-permute-start.2 = (bf16[2,128,512]{2,0,1:T(2,128)(2,1)S(1)}, bf16[2,128,512]{2,0,1:T(2,128)(2,1)S(1)}, u32[]{:S(2)}, u32[]{:S(2)}) collective-permute-start(bf16[2,128,512]{2,0,1:T(2,128)(2,1)S(1)} %convolution_convert_fusion.8), channel_id=1, source_target_pairs={{7,0},{0,1},{1,2},{2,3},{3,4},{4,5},{5,6},{6,7},{15,8},{8,9},{9,10... | collective-permute-start | bytes 786440 | tf_op jit(solution)/shard_map/while/body/eval_jaxpr/ppermute | solution.py:16
  91.8 13.7 %copy-start = (bf16[512,1024]{1,0:T(8,128)(2,1)S(1)}, bf16[512,1024]{1,0:T(8,128)(2,1)}, u32[]{:S(2)}) copy-start(bf16[512,1024]{1,0:T(8,128)(2,1)} %get-tuple-element.837) | copy-start | bytes 3145732 | tf_op jit(solution)/shard_map/while
  91.9 12.8 %collective-permute-start.1 = (bf16[2,128,512]{2,0,1:T(2,128)(2,1)S(1)}, bf16[2,128,512]{2,0,1:T(2,128)(2,1)S(1)}, u32[]{:S(2)}, u32[]{:S(2)}) collective-permute-start(bf16[2,128,512]{2,0,1:T(2,128)(2,1)S(1)} %convolution_convert_fusion.7), channel_id=1, source_target_pairs={{1,0},{2,1},{3,2},{4,3},{5,4},{6,5},{7,6},{0,7},{9,8},{10,9},{11,1... | collective-permute-start | bytes 786440 | tf_op jit(solution)/shard_map/while/body/eval_jaxpr/ppermute | solution.py:16
  115.5 8.7 %collective-permute-start = (bf16[256,512]{1,0:T(8,128)(2,1)S(1)}, bf16[256,512]{1,0:T(8,128)(2,1)S(1)}, u32[]{:S(2)}, u32[]{:S(2)}) collective-permute-start(bf16[256,512]{1,0:T(8,128)(2,1)S(1)} %get-tuple-element.801), channel_id=1, source_target_pairs={{8,0},{16,8},{24,16},{9,1},{17,9},{25,17},{10,2},{18,10},{26,18},{... | collective-permute-start | bytes 786440 | tf_op jit(solution)/shard_map/while/body/eval_jaxpr/ppermute | solution.py:10
  127.0 9.2 %collective-permute-start.2 = (bf16[2,128,512]{2,0,1:T(2,128)(2,1)S(1)}, bf16[2,128,512]{2,0,1:T(2,128)(2,1)S(1)}, u32[]{:S(2)}, u32[]{:S(2)}) collective-permute-start(bf16[2,128,512]{2,0,1:T(2,128)(2,1)S(1)} %convolution_convert_fusion.8), channel_id=1, source_target_pairs={{7,0},{0,1},{1,2},{2,3},{3,4},{4,5},{5,6},{6,7},{15,8},{8,9},{9,10... | collective-permute-start | bytes 786440 | tf_op jit(solution)/shard_map/while/body/eval_jaxpr/ppermute | solution.py:16
  127.8 9.3 %collective-permute-start.1 = (bf16[2,128,512]{2,0,1:T(2,128)(2,1)S(1)}, bf16[2,128,512]{2,0,1:T(2,128)(2,1)S(1)}, u32[]{:S(2)}, u32[]{:S(2)}) collective-permute-start(bf16[2,128,512]{2,0,1:T(2,128)(2,1)S(1)} %convolution_convert_fusion.7), channel_id=1, source_target_pairs={{1,0},{2,1},{3,2},{4,3},{5,4},{6,5},{7,6},{0,7},{9,8},{10,9},{11,1... | collective-permute-start | bytes 786440 | tf_op jit(solution)/shard_map/while/body/eval_jaxpr/ppermute | solution.py:16
  151.8 11.7 %collective-permute-start = (bf16[256,512]{1,0:T(8,128)(2,1)S(1)}, bf16[256,512]{1,0:T(8,128)(2,1)S(1)}, u32[]{:S(2)}, u32[]{:S(2)}) collective-permute-start(bf16[256,512]{1,0:T(8,128)(2,1)S(1)} %get-tuple-element.801), channel_id=1, source_target_pairs={{8,0},{16,8},{24,16},{9,1},{17,9},{25,17},{10,2},{18,10},{26,18},{... | collective-permute-start | bytes 786440 | tf_op jit(solution)/shard_map/while/body/eval_jaxpr/ppermute | solution.py:10
  166.3 9.2 %collective-permute-start.2 = (bf16[2,128,512]{2,0,1:T(2,128)(2,1)S(1)}, bf16[2,128,512]{2,0,1:T(2,128)(2,1)S(1)}, u32[]{:S(2)}, u32[]{:S(2)}) collective-permute-start(bf16[2,128,512]{2,0,1:T(2,128)(2,1)S(1)} %convolution_convert_fusion.8), channel_id=1, source_target_pairs={{7,0},{0,1},{1,2},{2,3},{3,4},{4,5},{5,6},{6,7},{15,8},{8,9},{9,10... | collective-permute-start | bytes 786440 | tf_op jit(solution)/shard_map/while/body/eval_jaxpr/ppermute | solution.py:16
  167.1 9.3 %collective-permute-start.1 = (bf16[2,128,512]{2,0,1:T(2,128)(2,1)S(1)}, bf16[2,128,512]{2,0,1:T(2,128)(2,1)S(1)}, u32[]{:S(2)}, u32[]{:S(2)}) collective-permute-start(bf16[2,128,512]{2,0,1:T(2,128)(2,1)S(1)} %convolution_convert_fusion.7), channel_id=1, source_target_pairs={{1,0},{2,1},{3,2},{4,3},{5,4},{6,5},{7,6},{0,7},{9,8},{10,9},{11,1... | collective-permute-start | bytes 786440 | tf_op jit(solution)/shard_map/while/body/eval_jaxpr/ppermute | solution.py:16
  191.1 12.5 %collective-permute-start = (bf16[256,512]{1,0:T(8,128)(2,1)S(1)}, bf16[256,512]{1,0:T(8,128)(2,1)S(1)}, u32[]{:S(2)}, u32[]{:S(2)}) collective-permute-start(bf16[256,512]{1,0:T(8,128)(2,1)S(1)} %get-tuple-element.801), channel_id=1, source_target_pairs={{8,0},{16,8},{24,16},{9,1},{17,9},{25,17},{10,2},{18,10},{26,18},{... | collective-permute-start | bytes 786440 | tf_op jit(solution)/shard_map/while/body/eval_jaxpr/ppermute | solution.py:10
  206.5 9.2 %collective-permute-start.2 = (bf16[2,128,512]{2,0,1:T(2,128)(2,1)S(1)}, bf16[2,128,512]{2,0,1:T(2,128)(2,1)S(1)}, u32[]{:S(2)}, u32[]{:S(2)}) collective-permute-start(bf16[2,128,512]{2,0,1:T(2,128)(2,1)S(1)} %convolution_convert_fusion.8), channel_id=1, source_target_pairs={{7,0},{0,1},{1,2},{2,3},{3,4},{4,5},{5,6},{6,7},{15,8},{8,9},{9,10... | collective-permute-start | bytes 786440 | tf_op jit(solution)/shard_map/while/body/eval_jaxpr/ppermute | solution.py:16
  207.3 9.3 %collective-permute-start.1 = (bf16[2,128,512]{2,0,1:T(2,128)(2,1)S(1)}, bf16[2,128,512]{2,0,1:T(2,128)(2,1)S(1)}, u32[]{:S(2)}, u32[]{:S(2)}) collective-permute-start(bf16[2,128,512]{2,0,1:T(2,128)(2,1)S(1)} %convolution_convert_fusion.7), channel_id=1, source_target_pairs={{1,0},{2,1},{3,2},{4,3},{5,4},{6,5},{7,6},{0,7},{9,8},{10,9},{11,1... | collective-permute-start | bytes 786440 | tf_op jit(solution)/shard_map/while/body/eval_jaxpr/ppermute | solution.py:16
  (39 other events, 122.5 us)
Sparse Core Ops, SparseCore 0:
  235.4 109.0 all-reduce.2
where the time goes:
time: 358 us; the launch traced here: 356 us
  waiting for transfers between devices  155 us (43%)
  other arithmetic  68.4 us (19%)
  local copies, waits for them, and re-layouts  45.2 us (13%)
  starting transfers between devices  37.9 us (11%)
  matrix products  34.3 us (10%)
  between operations  14.1 us (4%)
    psum x1, waiting for transfers between devices, shards(): lax.psum(final_state[2].astype(jnp.bfloat16), 'node').astype(jnp.float32)  109 us
    add x12, other arithmetic, advance(): return (new_grad, grads_out, first_sum + first_inc, second_sum + second_inc)  33.4 us
    ppermute x12, waiting for transfers between devices, passed_along(): return lax.ppermute(block, axis, route)  32.7 us
    ppermute x12, starting transfers between devices, passed_along(): return lax.ppermute(block, axis, route)  30.2 us
    ppermute x6, waiting for transfers between devices, shifted(): return lax.ppermute(block, axis, route)  12.8 us
    and x12, other arithmetic, picker(): return (place_mask & (selector & live_mask)[:, None]).astype(jnp.bfloat16)  11 us
    dynamic_slice x6, local copies, waits for them, and re-layouts, advance(): stored = lax.dynamic_index_in_dim(grads_out, group_safe, 0, keepdims=False)  10.5 us
    broadcast_in_dim x4, other arithmetic, shards(): return (final_state[1][None], first_total[None], second_total[None])  8.47 us
  transfers between devices with their start and end apart: 19, of which 16 were waited for; matrix products, arithmetic and copies ran while one was open for 13% of the time, Pallas kernels for 0%

commit v1 on v0

v1 whole, which is shorter than its diff:
```python
import functools

import jax
import jax.numpy as jnp
from jax import lax
from jax.experimental import pallas as pl
from jax.experimental.pallas import tpu as pltpu
from jax.sharding import PartitionSpec as P

MESH = pl.DeviceIdType.MESH
F32 = jnp.float32
BF16 = jnp.bfloat16
CHUNKS = 4
CONTRACT_LAST = (((1,), (1,)), ((), ()))
CONTRACT_FIRST = (((0,), (0,)), ((), ()))


def dot(a, b, dims=(((1,), (0,)), ((), ()))):
    return lax.dot_general(a, b, dims, preferred_element_type=F32)


def kernel(
    sections, nodes,
    rows_ref, cols_ref, ids_ref, count_ref, acts_ref, top_ref, w1_ref, w2_ref, table_ref,
    grads_ref, first_ref, second_ref,
    adj, g_in, to_next, to_prev, from_prev, from_next, act_s, slope_s, dm_s, dpre_s, acc1, acc2,
    send_x1, send_x2, recv_x1, recv_x2, send_z1, send_z2, recv_z1, recv_z2,
    term_ssem, term_rsem, hand_ssem, hand_rsem, x_ssem, x_rsem, z_ssem, z_rsem, az_ssem, az_rsem, ax_ssem, ax_rsem,
):
    groups, rows, feat = top_ref.shape
    hidden = w1_ref.shape[2]
    slots = rows_ref.shape[1]
    blk = table_ref.shape[-1]
    blocks = rows // blk
    sec = lax.axis_index("section")
    node = lax.axis_index("node")
    nxt = lax.rem(node + 1, nodes)
    prv = lax.rem(node + nodes - 1, nodes)
    line = nodes // 2
    along = node // 2
    side = lax.rem(node, 2)
    partner = node + 1 - 2 * side
    top_sec = sec == sections - 1
    has_below = sec > 0
    has_up = along < line - 1
    has_down = along > 0

    def remote(src, dst, ssem, rsem, node_to, sec_to=None):
        return pltpu.make_async_remote_copy(
            src_ref=src, dst_ref=dst, send_sem=ssem, recv_sem=rsem,
            device_id=(sec if sec_to is None else sec_to, node_to), device_id_type=MESH,
        )

    barrier = pltpu.get_barrier_semaphore()

    def greet(section_to, node_to):
        pl.semaphore_signal(barrier, inc=1, device_id=(section_to, node_to), device_id_type=MESH)

    greet(sec, nxt)
    greet(sec, prv)
    greet(sec, partner)
    pl.when(has_below)(lambda: greet(sec - 1, node))
    pl.when(jnp.logical_not(top_sec))(lambda: greet(sec + 1, node))
    pl.when(has_up)(lambda: greet(sec, node + 2))
    pl.when(has_down)(lambda: greet(sec, node - 2))

    def build(c):
        for d, owner in enumerate((node, nxt, prv)):
            for cb in range(blocks):
                col = owner * blocks + cb
                for r in range(blocks):
                    total = jnp.zeros((blk, blk), F32)
                    for k in range(slots):
                        live = (k < count_ref[c, 0]) & (rows_ref[c, k] == r) & (cols_ref[c, k] == col)
                        coef = jnp.where(live, 1.0, 0.0).astype(F32)
                        total = total + coef * table_ref[c, ids_ref[c, k]].astype(F32)
                    place = (d * blocks + cb) * blk
                    adj[c, place:place + blk, r * blk:(r + 1) * blk] = total.T.astype(BF16)

    def forward(c):
        h = acts_ref[0, c]
        step = hidden // 4
        for j in range(4):
            at = slice(j * step, (j + 1) * step)
            pre = dot(h, w1_ref[0, :, at])
            sigma = jax.nn.sigmoid(pre)
            act_s[c, :, at] = (pre * sigma).astype(BF16)
            slope_s[c, :, at] = sigma * (1.0 + pre * (1.0 - sigma))

    def weight_grads(c):
        def put(ref, at, value):
            if c == 0:
                ref[at, :] = value
            else:
                ref[at, :] += value

        step = hidden // 4
        for j in range(4):
            at = slice(j * step, (j + 1) * step)
            put(acc2, at, dot(act_s[c, :, at], dm_s[c], CONTRACT_FIRST))
        step = feat // 4
        for j in range(4):
            at = slice(j * step, (j + 1) * step)
            put(acc1, at, dot(acts_ref[0, c, :, at], dpre_s[c], CONTRACT_FIRST))

    def hand(c):
        return remote(grads_ref.at[0, c], g_in.at[c], hand_ssem.at[c], hand_rsem.at[c], node, sec - 1)

    build(0)
    greeted = 3 + has_below.astype(jnp.int32) + jnp.logical_not(top_sec).astype(jnp.int32)
    greeted = greeted + has_up.astype(jnp.int32) + has_down.astype(jnp.int32)
    pl.semaphore_wait(barrier, greeted)

    for c in range(groups):
        @pl.when(top_sec)
        def _():
            g_in[c] = top_ref[c]

        @pl.when(jnp.logical_not(top_sec))
        def _():
            hand(c).wait_recv()

        grad = g_in[c]
        to_next[c] = dot(adj[c, rows:2 * rows], grad).astype(BF16)
        ahead = remote(to_next.at[c], from_prev.at[c], term_ssem.at[c, 0], term_rsem.at[c, 0], nxt)
        ahead.start()
        to_prev[c] = dot(adj[c, 2 * rows:], grad).astype(BF16)
        back = remote(to_prev.at[c], from_next.at[c], term_ssem.at[c, 1], term_rsem.at[c, 1], prv)
        back.start()
        local = dot(adj[c, :rows], grad)
        forward(c)
        if c + 1 < groups:
            build(c + 1)
        if c > 0:
            weight_grads(c - 1)
        ahead.wait_recv()
        back.wait_recv()
        mid = (local + from_prev[c].astype(F32) + from_next[c].astype(F32)).astype(BF16)
        dm_s[c] = mid
        step = hidden // 4
        for j in range(4):
            at = slice(j * step, (j + 1) * step)
            dact = dot(mid, w2_ref[0, at, :], CONTRACT_LAST)
            dpre_s[c, :, at] = (dact * slope_s[c, :, at]).astype(BF16)
        new_grad = g_in[c].astype(F32) + dot(dpre_s[c], w1_ref[0], CONTRACT_LAST)
        grads_ref[0, c] = new_grad.astype(BF16)
        pl.when(has_below)(lambda: hand(c).start())

    weight_grads(groups - 1)
    half1 = feat // 2
    half2 = hidden // 2
    step1 = half1 // CHUNKS
    step2 = half2 // CHUNKS

    def own(kind, j):
        if kind == 0:
            return pl.ds(pl.multiple_of(side * half1 + j * step1, step1), step1)
        return pl.ds(pl.multiple_of(side * half2 + j * step2, step2), step2)

    def other(kind, j):
        if kind == 0:
            return pl.ds(pl.multiple_of((1 - side) * half1 + j * step1, step1), step1)
        return pl.ds(pl.multiple_of((1 - side) * half2 + j * step2, step2), step2)

    acc = (acc1, acc2)
    outs = (first_ref, second_ref)
    send_x, recv_x = (send_x1, send_x2), (recv_x1, recv_x2)
    send_z, recv_z = (send_z1, send_z2), (recv_z1, recv_z2)
    towards = (node + 2, node - 2)
    away = (node - 2, node + 2)
    has_towards = (has_up, has_down)
    has_away = (has_down, has_up)

    def x_copy(kind, j):
        return remote(
            send_x[kind].at[j], recv_x[kind].at[j], x_ssem.at[kind, j], x_rsem.at[kind, j], partner)

    def z_copy(kind, j):
        return remote(
            send_z[kind].at[j], recv_z[kind].at[j], z_ssem.at[kind, j], z_rsem.at[kind, j], towards[kind])

    def az_copy(kind, j):
        place = outs[kind].at[own(kind, j), :]
        return remote(place, place, az_ssem.at[kind, j], az_rsem.at[kind, j], away[kind])

    def ax_copy(kind, j):
        place = outs[kind].at[own(kind, j), :]
        return remote(place, place, ax_ssem.at[kind, j], ax_rsem.at[kind, j], partner)

    for j in range(CHUNKS):
        for kind in range(2):
            send_x[kind][j] = acc[kind][other(kind, j), :].astype(BF16)
            x_copy(kind, j).start()

    def reduce_chunk(kind, j):
        x_copy(kind, j).wait_recv()
        value = acc[kind][own(kind, j), :] + recv_x[kind][j].astype(F32)
        send_z[kind][j] = value.astype(BF16)

        @pl.when(has_away[kind])
        def _():
            z_copy(kind, j).wait_recv()
            send_z[kind][j] = (value + recv_z[kind][j].astype(F32)).astype(BF16)

        @pl.when(has_towards[kind])
        def _():
            z_copy(kind, j).start()

        @pl.when(jnp.logical_not(has_towards[kind]))
        def _():
            outs[kind][own(kind, j), :] = send_z[kind][j]
            az_copy(kind, j).start()
            ax_copy(kind, j).start()

    def gather_chunk(kind, j):
        @pl.when(has_towards[kind])
        def _():
            az_copy(kind, j).wait_recv()
            pl.when(has_away[kind])(lambda: az_copy(kind, j).start())
            ax_copy(kind, j).start()

    def in_order(step):
        def run(first):
            for kind in (first, 1 - first):
                for j in range(CHUNKS):
                    step(kind, j)

        return run

    early = along < line // 2
    late = jnp.logical_not(early)
    pl.when(early)(lambda: in_order(reduce_chunk)(0))
    pl.when(late)(lambda: in_order(reduce_chunk)(1))
    pl.when(early)(lambda: in_order(gather_chunk)(1))
    pl.when(late)(lambda: in_order(gather_chunk)(0))

    for kind in range(2):
        for j in range(CHUNKS):
            ax_copy(kind, j).wait()
            x_copy(kind, j).wait_send()
            pl.when(has_towards[kind])(lambda: z_copy(kind, j).wait_send())
            pl.when(has_away[kind])(lambda: az_copy(kind, j).wait_send())
    for c in range(groups):
        remote(to_next.at[c], from_prev.at[c], term_ssem.at[c, 0], term_rsem.at[c, 0], nxt).wait_send()
        remote(to_prev.at[c], from_next.at[c], term_ssem.at[c, 1], term_rsem.at[c, 1], prv).wait_send()
        pl.when(has_below)(lambda: hand(c).wait_send())


def shards(acts, top_grad, w_in, w_out, tile_table, tile_rows, tile_cols, tile_ids, tile_count):
    sections = lax.axis_size("section")
    nodes = lax.axis_size("node")
    groups, rows, feat = top_grad.shape
    hidden = w_in.shape[2]
    vmem = pl.BlockSpec(memory_space=pltpu.VMEM)
    smem = pl.BlockSpec(memory_space=pltpu.SMEM)
    wide = lambda kind, count: pltpu.VMEM((groups, rows, count), kind)
    part1 = pltpu.VMEM((CHUNKS, feat // 2 // CHUNKS, hidden), BF16)
    part2 = pltpu.VMEM((CHUNKS, hidden // 2 // CHUNKS, feat), BF16)
    dma = pltpu.SemaphoreType.DMA
    grads, first, second = pl.pallas_call(
        functools.partial(kernel, sections, nodes),
        out_shape=(
            jax.ShapeDtypeStruct((1, groups, rows, feat), BF16),
            jax.ShapeDtypeStruct((feat, hidden), BF16),
            jax.ShapeDtypeStruct((hidden, feat), BF16),
        ),
        in_specs=[smem] * 4 + [vmem] * 5,
        out_specs=(vmem, vmem, vmem),
        scratch_shapes=[
            pltpu.VMEM((groups, 3 * rows, rows), BF16),
            *[wide(BF16, feat)] * 5,
            wide(BF16, hidden),
            wide(F32, hidden),
            wide(BF16, feat),
            wide(BF16, hidden),
            pltpu.VMEM((feat, hidden), F32),
            pltpu.VMEM((hidden, feat), F32),
            *[part1, part2] * 4,
            dma((groups, 2)), dma((groups, 2)), dma((groups,)), dma((groups,)),
            *[dma((2, CHUNKS))] * 8,
        ],
        compiler_params=pltpu.CompilerParams(
            collective_id=0, has_side_effects=True, vmem_limit_bytes=48 * 1024 * 1024
        ),
        name="relay_back",
    )(tile_rows, tile_cols, tile_ids, tile_count, acts, top_grad, w_in, w_out, tile_table)
    return grads, first.astype(F32)[None], second.astype(F32)[None]


def solution(mesh):
    return jax.shard_map(
        shards,
        mesh=mesh,
        in_specs=(
            P("section", None, "node", None),
            P(None, "node", None),
            P("section", None, None),
            P("section", None, None),
            P(None, "node", None, None),
            P(None, "node"),
            P(None, "node"),
            P(None, "node"),
            P(None, "node"),
        ),
        out_specs=(
            P("section", None, "node", None),
            P("section", None, None),
            P("section", None, None),
        ),
        check_vma=False,
    )
```

time: 358 us -> 150 us (0.42)
  waiting for transfers between devices: 155 us -> 0 us
  Pallas kernels: 0 us -> 139 us
  other arithmetic: 68.4 us -> 3.18 us
  local copies, waits for them, and re-layouts: 45.2 us -> 7.06 us
  starting transfers between devices: 37.9 us -> 0 us
  matrix products: 34.3 us -> 0 us
  between operations: 14.1 us -> 0.65 us
    pallas_call x0 -> x1, Pallas kernels: none -> 139 us  [shards(): pl.pallas_call(functools.partial(kernel, sections, nodes), out_shape=(jax...]
    psum x1 -> x0, waiting for transfers between devices: 109 us -> none  [shards(): lax.psum(final_state[2].astype(jnp.bfloat16), 'node').astype(jnp.float32)]
    ppermute x18 -> x0, waiting for transfers between devices: 45.5 us -> none  [the longest x12 32.7 us: passed_along(): return lax.ppermute(block, axis, route)]
    ppermute x18 -> x0, starting transfers between devices: 37.9 us -> none  [the longest x12 30.2 us: passed_along(): return lax.ppermute(block, axis, route)]
    dot_general x39 -> x0, matrix products: 34.3 us -> none  [the longest x3 5.57 us: mlp_back(): lax.dot_general(act_val, grad_mid, (((0,), (0,)), ((), ())), preferred_el...]
    add x12 -> x0, other arithmetic: 33.4 us -> none  [advance(): return (new_grad, grads_out, first_sum + first_inc, second_sum + second_inc)]
    dynamic_slice x12 -> x0, local copies, waits for them, and re-layouts: 17.9 us -> none  [the longest x6 10.5 us: advance(): stored = lax.dynamic_index_in_dim(grads_out, group_safe, 0, keepdims=False)]
    and x12 -> x0, other arithmetic: 11 us -> none  [picker(): return (place_mask & (selector & live_mask)[:, None]).astype(jnp.bfloat16)]
  transfers between devices with their start and end apart: 19 -> 0, of which waited for: 16 -> 0; matrix products, arithmetic and copies ran while one was open for 13% -> 0% of each run, Pallas kernels for 0% -> 0%
where the time goes in v1:
time: 150 us
  Pallas kernels  139 us (93%)
  local copies, waits for them, and re-layouts  7.06 us (5%)
  other arithmetic  3.18 us (2%)
    pallas_call x1, Pallas kernels, shards(): pl.pallas_call(functools.partial(kernel, sections, nodes), out_shape=(jax...  139 us
    unnamed x14, local copies, waits for them, and re-layouts  7.06 us
    broadcast_in_dim x2, other arithmetic, shards(): return (grads, first.astype(F32)[None], second.astype(F32)[None])  3.18 us

profile of v1, /device:TPU:0, one launch (start us, length us, event | category | flops | bytes accessed | tf_op | source)
XLA Modules:
  0.0 150.1 jit_solution(16078214690877783228)
XLA Ops:
  0.6 0.7 copy.12.count_ref
  1.4 0.0 copy-start
  1.4 1.1 copy-done
  2.5 0.0 copy-start.1
  2.5 1.1 copy-done.1
  3.6 0.0 copy-start.2
  3.6 1.1 copy-done.2
  4.8 0.0 copy-start.3
  4.8 0.7 copy-done.3
  5.5 0.0 copy-start.4
  5.5 0.7 copy-done.4
  6.1 0.0 copy-start.5
  6.1 0.7 copy-done.5
  6.8 139.2 %relay_back.1 = (bf16[1,3,256,512]{3,2,1,0:T(8,128)(2,1)S(1)}, bf16[512,1024]{1,0:T(8,128)(2,1)S(1)}, bf16[1024,512]{1,0:T(8,128)(2,1)S(1)}) custom-call(s32[3,8]{1,0:T(4,128)S(1)} %copy-done.3, s32[3,8]{1,0:T(4,128)S(1)} %copy-done.4, s32[3,8]{1,0:T(4,128)S(1)} %copy-done.5, s32[3,1]{1,0:T(4,128)S(1)} %copy.12.count_ref, ...), custom_call_target="tpu_custom_call" | custom-call | tf_op jit(solution)/shard_map/relay_back/pallas_call | solution.py:260
  146.1 1.6 %bitcast_convert_fusion.1 = f32[1,512,1024]{2,1,0:T(8,128)} fusion(bf16[512,1024]{1,0:T(8,128)(2,1)S(1)} %get-tuple-element.7), kind=kLoop, calls=%fused_computation.1 | loop fusion | flops 524288 | bytes 3145728 | tf_op jit(solution)/shard_map/broadcast_in_dim | solution.py:287
  147.6 1.6 %bitcast_convert_fusion = f32[1,1024,512]{2,1,0:T(8,128)} fusion(bf16[1024,512]{1,0:T(8,128)(2,1)S(1)} %get-tuple-element.8), kind=kLoop, calls=%fused_computation | loop fusion | flops 524288 | bytes 3145728 | tf_op jit(solution)/shard_map/broadcast_in_dim | solution.py:287
  149.2 0.9 copy.14
Async XLA Ops:
  1.4 1.1 copy-start
  2.5 1.1 copy-start.1
  3.6 1.1 copy-start.2
  4.8 0.7 copy-start.3
  5.5 0.7 copy-start.4
  6.1 0.7 copy-start.5

commit v2 on v1

--- a/solution.py
+++ b/solution.py
@@ -11,6 +11,7 @@
 F32 = jnp.float32
 BF16 = jnp.bfloat16
 CHUNKS = 4
+HALVES = 2
 CONTRACT_LAST = (((1,), (1,)), ((), ()))
 CONTRACT_FIRST = (((0,), (0,)), ((), ()))
 
@@ -21,27 +22,34 @@
 
 def kernel(
     sections, nodes,
-    rows_ref, cols_ref, ids_ref, count_ref, acts_ref, top_ref, w1_ref, w2_ref, table_ref,
+    rows_ref, cols_ref, ids_ref, count_ref, acts_hbm, top_hbm, w1_hbm, w2_hbm, table_hbm,
     grads_ref, first_ref, second_ref,
-    adj, g_in, to_next, to_prev, from_prev, from_next, act_s, slope_s, dm_s, dpre_s, acc1, acc2,
+    acts_ref, top_ref, w1_ref, w2_ref, table_ref, load_sem,
+    adj_own, adj_out, adj_par, g_own, g_par, g_out, to_line, from_line, act_s, slope_s, dm_s, dpre_s, acc1, acc2,
     send_x1, send_x2, recv_x1, recv_x2, send_z1, send_z2, recv_z1, recv_z2,
-    term_ssem, term_rsem, hand_ssem, hand_rsem, x_ssem, x_rsem, z_ssem, z_rsem, az_ssem, az_rsem, ax_ssem, ax_rsem,
+    adj_ssem, adj_rsem, pass_ssem, own_ssem, own_rsem, par_ssem, par_rsem, term_ssem, term_rsem,
+    x_ssem, x_rsem, z_ssem, z_rsem, az_ssem, az_rsem, ax_ssem, ax_rsem,
 ):
-    groups, rows, feat = top_ref.shape
+    groups, halves, rows, width = g_own.shape
+    feat = halves * width
     hidden = w1_ref.shape[2]
     slots = rows_ref.shape[1]
     blk = table_ref.shape[-1]
     blocks = rows // blk
     sec = lax.axis_index("section")
     node = lax.axis_index("node")
-    nxt = lax.rem(node + 1, nodes)
-    prv = lax.rem(node + nodes - 1, nodes)
     line = nodes // 2
     along = node // 2
     side = lax.rem(node, 2)
     partner = node + 1 - 2 * side
+    outer = lax.rem(node + nodes - 1 + 2 * side, nodes)
+    line_to = lax.rem(node + 2 + side * (nodes - 4), nodes)
+    line_from = lax.rem(node + nodes - 2 + side * (4 - nodes) + side * nodes, nodes)
     top_sec = sec == sections - 1
+    below_top = sec < sections - 1
     has_below = sec > 0
+    odd = lax.rem(sec, 2) == 1
+    even = lax.rem(sec, 2) == 0
     has_up = along < line - 1
     has_down = along > 0
 
@@ -56,33 +64,81 @@
     def greet(section_to, node_to):
         pl.semaphore_signal(barrier, inc=1, device_id=(section_to, node_to), device_id_type=MESH)
 
-    greet(sec, nxt)
-    greet(sec, prv)
     greet(sec, partner)
+    greet(sec, line_to)
+    greet(sec, line_from)
+    pl.when(odd)(lambda: greet(sec - 1, partner))
+    pl.when(even)(lambda: greet(sec + 1, partner))
     pl.when(has_below)(lambda: greet(sec - 1, node))
-    pl.when(jnp.logical_not(top_sec))(lambda: greet(sec + 1, node))
-    pl.when(has_up)(lambda: greet(sec, node + 2))
-    pl.when(has_down)(lambda: greet(sec, node - 2))
+    pl.when(below_top)(lambda: greet(sec + 1, node))
+
+    def load(at, src, dst):
+        return pltpu.make_async_copy(src, dst, load_sem.at[at])
+
+    load_table = load(0, table_hbm, table_ref)
+    load_acts = load(1, acts_hbm, acts_ref)
+    load_w1 = load(2, w1_hbm, w1_ref)
+    load_w2 = load(3, w2_hbm, w2_ref)
+    load_table.start()
+    pl.when(top_sec)(lambda: load(4, top_hbm, top_ref).start())
+    load_acts.start()
+    load_w1.start()
+    load_w2.start()
+
+    def block(c, owner, cb, r):
+        total = jnp.zeros((blk, blk), F32)
+        for k in range(slots):
+            live = (k < count_ref[c, 0]) & (rows_ref[c, k] == r) & (cols_ref[c, k] == owner * blocks + cb)
+            coef = jnp.where(live, 1.0, 0.0).astype(F32)
+            total = total + coef * table_ref[c, ids_ref[c, k]].astype(F32)
+        return total.T.astype(BF16)
+
+    def adj_copy(c):
+        return remote(adj_out.at[c], adj_par.at[c], adj_ssem.at[c], adj_rsem.at[c], partner)
+
+    def pass_copy(c):
+        return remote(adj_par.at[c], adj_par.at[c], pass_ssem.at[c], adj_rsem.at[c], node, sec - 1)
+
+    def own_copy(c, f):
+        return remote(
+            g_out.at[c, f], g_own.at[c, f], own_ssem.at[c, f], own_rsem.at[c, f], node, sec - 1)
+
+    def par_copy(c, f):
+        return remote(
+            g_out.at[c, f], g_par.at[c, f], par_ssem.at[c, f], par_rsem.at[c, f], partner, sec - 1)
+
+    def relay_copy(c, f):
+        return remote(
+            g_own.at[c, f], g_par.at[c, f], par_ssem.at[groups + c, f], par_rsem.at[c, f], partner)
+
+    def line_copy(c, f):
+        return remote(
+            to_line.at[c, f], from_line.at[c, f], term_ssem.at[c, f], term_rsem.at[c, f], line_to)
 
     def build(c):
-        for d, owner in enumerate((node, nxt, prv)):
-            for cb in range(blocks):
-                col = owner * blocks + cb
-                for r in range(blocks):
-                    total = jnp.zeros((blk, blk), F32)
-                    for k in range(slots):
-                        live = (k < count_ref[c, 0]) & (rows_ref[c, k] == r) & (cols_ref[c, k] == col)
-                        coef = jnp.where(live, 1.0, 0.0).astype(F32)
-                        total = total + coef * table_ref[c, ids_ref[c, k]].astype(F32)
-                    place = (d * blocks + cb) * blk
-                    adj[c, place:place + blk, r * blk:(r + 1) * blk] = total.T.astype(BF16)
+        @pl.when(odd)
+        def _():
+            for d, owner in enumerate((partner, outer)):
+                for cb in range(blocks):
+                    for r in range(blocks):
+                        place = (d * blocks + cb) * blk
+                        adj_out[c, place:place + blk, r * blk:(r + 1) * blk] = block(c, owner, cb, r)
+            adj_copy(c).start()
+
+        for cb in range(blocks):
+            for r in range(blocks):
+                adj_own[c, cb * blk:(cb + 1) * blk, r * blk:(r + 1) * blk] = block(c, node, cb, r)
+
+    def take_top(c):
+        for f in range(halves):
+            g_own[c, f] = top_ref[c, :, f * width:(f + 1) * width]
+            relay_copy(c, f).start()
 
     def forward(c):
-        h = acts_ref[0, c]
         step = hidden // 4
         for j in range(4):
             at = slice(j * step, (j + 1) * step)
-            pre = dot(h, w1_ref[0, :, at])
+            pre = dot(acts_ref[0, c], w1_ref[0, :, at])
             sigma = jax.nn.sigmoid(pre)
             act_s[c, :, at] = (pre * sigma).astype(BF16)
             slope_s[c, :, at] = sigma * (1.0 + pre * (1.0 - sigma))
@@ -103,48 +159,67 @@
             at = slice(j * step, (j + 1) * step)
             put(acc1, at, dot(acts_ref[0, c, :, at], dpre_s[c], CONTRACT_FIRST))
 
-    def hand(c):
-        return remote(grads_ref.at[0, c], g_in.at[c], hand_ssem.at[c], hand_rsem.at[c], node, sec - 1)
-
+    greeted = 4 + has_below.astype(jnp.int32) + below_top.astype(jnp.int32)
+    pl.semaphore_wait(barrier, greeted)
+
+    @pl.when(top_sec)
+    def _():
+        load(4, top_hbm, top_ref).wait()
+        take_top(0)
+
+    load_table.wait()
     build(0)
-    greeted = 3 + has_below.astype(jnp.int32) + jnp.logical_not(top_sec).astype(jnp.int32)
-    greeted = greeted + has_up.astype(jnp.int32) + has_down.astype(jnp.int32)
-    pl.semaphore_wait(barrier, greeted)
+    load_acts.wait()
+    load_w1.wait()
+    load_w2.wait()
+
+    @pl.when(below_top)
+    def _():
+        for c in range(1, groups):
+            build(c)
+        for c in range(groups):
+            forward(c)
 
     for c in range(groups):
+        @pl.when(below_top)
+        def _():
+            for f in range(halves):
+                own_copy(c, f).wait_recv()
+                pl.when(odd)(lambda: relay_copy(c, f).start())
+
+        local = [dot(adj_own[c], g_own[c, f]) for f in range(halves)]
+        adj_copy(c).wait_recv()
+        pl.when(odd)(lambda: pass_copy(c).start())
+        for f in range(halves):
+            par_copy(c, f).wait_recv()
+            to_line[c, f] = dot(adj_par[c, rows:], g_par[c, f]).astype(BF16)
+            line_copy(c, f).start()
+            local[f] = local[f] + dot(adj_par[c, :rows], g_par[c, f])
+
         @pl.when(top_sec)
         def _():
-            g_in[c] = top_ref[c]
-
-        @pl.when(jnp.logical_not(top_sec))
-        def _():
-            hand(c).wait_recv()
-
-        grad = g_in[c]
-        to_next[c] = dot(adj[c, rows:2 * rows], grad).astype(BF16)
-        ahead = remote(to_next.at[c], from_prev.at[c], term_ssem.at[c, 0], term_rsem.at[c, 0], nxt)
-        ahead.start()
-        to_prev[c] = dot(adj[c, 2 * rows:], grad).astype(BF16)
-        back = remote(to_prev.at[c], from_next.at[c], term_ssem.at[c, 1], term_rsem.at[c, 1], prv)
-        back.start()
-        local = dot(adj[c, :rows], grad)
-        forward(c)
-        if c + 1 < groups:
-            build(c + 1)
+            if c + 1 < groups:
+                take_top(c + 1)
+                build(c + 1)
+            forward(c)
+
         if c > 0:
             weight_grads(c - 1)
-        ahead.wait_recv()
-        back.wait_recv()
-        mid = (local + from_prev[c].astype(F32) + from_next[c].astype(F32)).astype(BF16)
-        dm_s[c] = mid
+        for f in range(halves):
+            line_copy(c, f).wait_recv()
+            dm_s[c, :, f * width:(f + 1) * width] = (local[f] + from_line[c, f].astype(F32)).astype(BF16)
         step = hidden // 4
         for j in range(4):
             at = slice(j * step, (j + 1) * step)
-            dact = dot(mid, w2_ref[0, at, :], CONTRACT_LAST)
+            dact = dot(dm_s[c], w2_ref[0, at, :], CONTRACT_LAST)
             dpre_s[c, :, at] = (dact * slope_s[c, :, at]).astype(BF16)
-        new_grad = g_in[c].astype(F32) + dot(dpre_s[c], w1_ref[0], CONTRACT_LAST)
-        grads_ref[0, c] = new_grad.astype(BF16)
-        pl.when(has_below)(lambda: hand(c).start())
+        for f in range(halves):
+            at = slice(f * width, (f + 1) * width)
+            back = dot(dpre_s[c], w1_ref[0, at, :], CONTRACT_LAST)
+            g_out[c, f] = (g_own[c, f].astype(F32) + back).astype(BF16)
+            pl.when(has_below)(lambda: own_copy(c, f).start())
+            pl.when(odd)(lambda: par_copy(c, f).start())
+            grads_ref[0, c, :, at] = g_out[c, f]
 
     weight_grads(groups - 1)
     half1 = feat // 2
@@ -241,9 +316,19 @@
             pl.when(has_towards[kind])(lambda: z_copy(kind, j).wait_send())
             pl.when(has_away[kind])(lambda: az_copy(kind, j).wait_send())
     for c in range(groups):
-        remote(to_next.at[c], from_prev.at[c], term_ssem.at[c, 0], term_rsem.at[c, 0], nxt).wait_send()
-        remote(to_prev.at[c], from_next.at[c], term_ssem.at[c, 1], term_rsem.at[c, 1], prv).wait_send()
-        pl.when(has_below)(lambda: hand(c).wait_send())
+        @pl.when(odd)
+        def _():
+            adj_copy(c).wait_send()
+            pass_copy(c).wait_send()
+
+        for f in range(halves):
+            line_copy(c, f).wait_send()
+            pl.when(has_below)(lambda: own_copy(c, f).wait_send())
+
+            @pl.when(odd)
+            def _():
+                par_copy(c, f).wait_send()
+                relay_copy(c, f).wait_send()
 
 
 def shards(acts, top_grad, w_in, w_out, tile_table, tile_rows, tile_cols, tile_ids, tile_count):
@@ -252,7 +337,10 @@
     groups, rows, feat = top_grad.shape
     hidden = w_in.shape[2]
     vmem = pl.BlockSpec(memory_space=pltpu.VMEM)
+    hbm = pl.BlockSpec(memory_space=pltpu.HBM)
     smem = pl.BlockSpec(memory_space=pltpu.SMEM)
+    width = feat // HALVES
+    half = pltpu.VMEM((groups, HALVES, rows, width), BF16)
     wide = lambda kind, count: pltpu.VMEM((groups, rows, count), kind)
     part1 = pltpu.VMEM((CHUNKS, feat // 2 // CHUNKS, hidden), BF16)
     part2 = pltpu.VMEM((CHUNKS, hidden // 2 // CHUNKS, feat), BF16)
@@ -264,11 +352,14 @@
             jax.ShapeDtypeStruct((feat, hidden), BF16),
             jax.ShapeDtypeStruct((hidden, feat), BF16),
         ),
-        in_specs=[smem] * 4 + [vmem] * 5,
+        in_specs=[smem] * 4 + [hbm] * 5,
         out_specs=(vmem, vmem, vmem),
         scratch_shapes=[
-            pltpu.VMEM((groups, 3 * rows, rows), BF16),
-            *[wide(BF16, feat)] * 5,
+            *[pltpu.VMEM(arg.shape, BF16) for arg in (acts, top_grad, w_in, w_out, tile_table)],
+            dma((5,)),
+            pltpu.VMEM((groups, rows, rows), BF16),
+            *[pltpu.VMEM((groups, 2 * rows, rows), BF16)] * 2,
+            *[half] * 5,
             wide(BF16, hidden),
             wide(F32, hidden),
             wide(BF16, feat),
@@ -276,7 +367,10 @@
             pltpu.VMEM((feat, hidden), F32),
             pltpu.VMEM((hidden, feat), F32),
             *[part1, part2] * 4,
-            dma((groups, 2)), dma((groups, 2)), dma((groups,)), dma((groups,)),
+            *[dma((groups,))] * 3,
+            *[dma((groups, HALVES))] * 2,
+            dma((2 * groups, HALVES)),
+            *[dma((groups, HALVES))] * 3,
             *[dma((2, CHUNKS))] * 8,
         ],
         compiler_params=pltpu.CompilerParams(

time: 150 us -> 144 us (0.960)
  Pallas kernels: 139 us -> 133 us
    pallas_call x1, Pallas kernels: 139 us -> 133 us  [shards(): pl.pallas_call(functools.partial(kernel, sections, nodes), out_shape=(jax...]
where the time goes in v2:
time: 144 us
  Pallas kernels  133 us (92%)
  local copies, waits for them, and re-layouts  7.06 us (5%)
  other arithmetic  3.18 us (2%)
    pallas_call x1, Pallas kernels, shards(): pl.pallas_call(functools.partial(kernel, sections, nodes), out_shape=(jax...  133 us
    unnamed x14, local copies, waits for them, and re-layouts  7.06 us
    broadcast_in_dim x2, other arithmetic, shards(): return (grads, first.astype(F32)[None], second.astype(F32)[None])  3.18 us

profile of v2, /device:TPU:0, one launch (start us, length us, event | category | flops | bytes accessed | tf_op | source)
XLA Modules:
  0.0 143.5 jit_solution(13151565357328073243)
XLA Ops:
  0.6 0.7 copy.12.count_ref
  1.4 0.0 copy-start
  1.4 1.1 copy-done
  2.5 0.0 copy-start.1
  2.5 1.1 copy-done.1
  3.6 0.0 copy-start.2
  3.6 1.1 copy-done.2
  4.8 0.0 copy-start.3
  4.8 0.7 copy-done.3
  5.5 0.0 copy-start.4
  5.5 0.7 copy-done.4
  6.1 0.0 copy-start.5
  6.1 0.7 copy-done.5
  6.8 132.6 %relay_back.1 = (bf16[1,3,256,512]{3,2,1,0:T(8,128)(2,1)S(1)}, bf16[512,1024]{1,0:T(8,128)(2,1)S(1)}, bf16[1024,512]{1,0:T(8,128)(2,1)S(1)}) custom-call(s32[3,8]{1,0:T(4,128)S(1)} %copy-done.3, s32[3,8]{1,0:T(4,128)S(1)} %copy-done.4, s32[3,8]{1,0:T(4,128)S(1)} %copy-done.5, s32[3,1]{1,0:T(4,128)S(1)} %copy.12.count_ref, ...), custom_call_target="tpu_custom_call" | custom-call | tf_op jit(solution)/shard_map/relay_back/pallas_call | solution.py:348
  139.5 1.6 %bitcast_convert_fusion.1 = f32[1,512,1024]{2,1,0:T(8,128)} fusion(bf16[512,1024]{1,0:T(8,128)(2,1)S(1)} %get-tuple-element.7), kind=kLoop, calls=%fused_computation.1 | loop fusion | flops 524288 | bytes 3145728 | tf_op jit(solution)/shard_map/broadcast_in_dim | solution.py:381
  141.0 1.6 %bitcast_convert_fusion = f32[1,1024,512]{2,1,0:T(8,128)} fusion(bf16[1024,512]{1,0:T(8,128)(2,1)S(1)} %get-tuple-element.8), kind=kLoop, calls=%fused_computation | loop fusion | flops 524288 | bytes 3145728 | tf_op jit(solution)/shard_map/broadcast_in_dim | solution.py:381
  142.6 0.9 copy.14
Async XLA Ops:
  1.4 1.1 copy-start
  2.5 1.1 copy-start.1
  3.6 1.1 copy-start.2
  4.8 0.7 copy-start.3
  5.5 0.7 copy-start.4
  6.1 0.7 copy-start.5

commit v3 on v2

--- a/solution.py
+++ b/solution.py
@@ -10,7 +10,8 @@
 MESH = pl.DeviceIdType.MESH
 F32 = jnp.float32
 BF16 = jnp.bfloat16
-CHUNKS = 4
+CHUNKS = 8
+AHEAD = 3
 HALVES = 2
 CONTRACT_LAST = (((1,), (1,)), ((), ()))
 CONTRACT_FIRST = (((0,), (0,)), ((), ()))
@@ -262,13 +263,11 @@
         place = outs[kind].at[own(kind, j), :]
         return remote(place, place, ax_ssem.at[kind, j], ax_rsem.at[kind, j], partner)
 
-    for j in range(CHUNKS):
-        for kind in range(2):
-            send_x[kind][j] = acc[kind][other(kind, j), :].astype(BF16)
-            x_copy(kind, j).start()
+    def send_across(kind, j):
+        send_x[kind][j] = acc[kind][other(kind, j), :].astype(BF16)
+        x_copy(kind, j).start()
 
     def reduce_chunk(kind, j):
-        x_copy(kind, j).wait_recv()
         value = acc[kind][own(kind, j), :] + recv_x[kind][j].astype(F32)
         send_z[kind][j] = value.astype(BF16)
 
@@ -294,20 +293,27 @@
             pl.when(has_away[kind])(lambda: az_copy(kind, j).start())
             ax_copy(kind, j).start()
 
-    def in_order(step):
-        def run(first):
-            for kind in (first, 1 - first):
-                for j in range(CHUNKS):
-                    step(kind, j)
-
-        return run
+    def reduce_all(first):
+        order = [(kind, j) for kind in (first, 1 - first) for j in range(CHUNKS)]
+        for kind, j in order[:AHEAD]:
+            send_across(kind, j)
+        for i, (kind, j) in enumerate(order):
+            x_copy(kind, j).wait_recv()
+            if i + AHEAD < len(order):
+                send_across(*order[i + AHEAD])
+            reduce_chunk(kind, j)
+
+    def gather_all(first):
+        for kind in (first, 1 - first):
+            for j in range(CHUNKS):
+                gather_chunk(kind, j)
 
     early = along < line // 2
     late = jnp.logical_not(early)
-    pl.when(early)(lambda: in_order(reduce_chunk)(0))
-    pl.when(late)(lambda: in_order(reduce_chunk)(1))
-    pl.when(early)(lambda: in_order(gather_chunk)(1))
-    pl.when(late)(lambda: in_order(gather_chunk)(0))
+    pl.when(early)(lambda: reduce_all(0))
+    pl.when(late)(lambda: reduce_all(1))
+    pl.when(early)(lambda: gather_all(1))
+    pl.when(late)(lambda: gather_all(0))
 
     for kind in range(2):
         for j in range(CHUNKS):
@@ -374,7 +380,7 @@
             *[dma((2, CHUNKS))] * 8,
         ],
         compiler_params=pltpu.CompilerParams(
-            collective_id=0, has_side_effects=True, vmem_limit_bytes=48 * 1024 * 1024
+            collective_id=0, has_side_effects=True, vmem_limit_bytes=62 * 1024 * 1024
         ),
         name="relay_back",
     )(tile_rows, tile_cols, tile_ids, tile_count, acts, top_grad, w_in, w_out, tile_table)

time: 144 us -> 140 us (0.972)
  local copies, waits for them, and re-layouts: 7.06 us -> 2.2 us
    unnamed x14 -> x6, local copies, waits for them, and re-layouts: 7.06 us -> 2.2 us
where the time goes in v3:
time: 140 us; the launch traced here: 139 us
  Pallas kernels  132 us (94%)
  other arithmetic  4.49 us (3%)
  local copies, waits for them, and re-layouts  2.2 us (2%)
    pallas_call x1, Pallas kernels, shards(): pl.pallas_call(functools.partial(kernel, sections, nodes), out_shape=(jax...  132 us
    broadcast_in_dim x2, other arithmetic, shards(): return (grads, first.astype(F32)[None], second.astype(F32)[None])  4.49 us

profile of v3, /device:TPU:0, one launch (start us, length us, event | category | flops | bytes accessed | tf_op | source)
XLA Modules:
  0.0 139.4 jit_solution(5203296393523588160)
XLA Ops:
  0.6 1.3 copy.12.count_ref
  1.9 132.0 %relay_back.1 = (bf16[1,3,256,512]{3,2,1,0:T(8,128)(2,1)}, bf16[512,1024]{1,0:T(8,128)(2,1)}, bf16[1024,512]{1,0:T(8,128)(2,1)}) custom-call(s32[3,8]{1,0:T(4,128)} %rows_ref.1, s32[3,8]{1,0:T(4,128)} %cols_ref.1, s32[3,8]{1,0:T(4,128)} %ids_ref.1, s32[3,1]{1,0:T(4,128)} %copy.12.count_ref, bf16[1,3,256,512]{3,2,1,0:T(8,128)(2,1)} %acts_hbm.1, ...), custom_call_target="tpu_custom_call" | custom-call | tf_op jit(solution)/shard_map/relay_back/pallas_call | solution.py:354
  134.0 0.0 copy-start
  134.0 2.9 %bitcast_convert_fusion.1 = f32[1,512,1024]{2,1,0:T(8,128)} fusion(bf16[512,1024]{1,0:T(8,128)(2,1)} %get-tuple-element.7), kind=kLoop, calls=%fused_computation.1 | loop fusion | flops 524288 | bytes 3145728 | tf_op jit(solution)/shard_map/broadcast_in_dim | solution.py:387
  136.9 0.0 copy-done
  136.9 0.0 copy-start.1
  136.9 1.6 %bitcast_convert_fusion = f32[1,1024,512]{2,1,0:T(8,128)} fusion(bf16[1024,512]{1,0:T(8,128)(2,1)S(1)} %copy-done), kind=kLoop, calls=%fused_computation | loop fusion | flops 524288 | bytes 3145728 | tf_op jit(solution)/shard_map/broadcast_in_dim | solution.py:387
  138.5 0.0 copy-done.1
  138.5 0.9 copy.14
Async XLA Ops:
  134.0 2.9 %copy-start = (bf16[1024,512]{1,0:T(8,128)(2,1)S(1)}, bf16[1024,512]{1,0:T(8,128)(2,1)}, u32[]{:S(2)}) copy-start(bf16[1024,512]{1,0:T(8,128)(2,1)} %get-tuple-element.8) | copy-start | bytes 3145732
  136.9 1.6 %copy-start.1 = (bf16[1,3,256,512]{3,2,1,0:T(8,128)(2,1)S(1)}, bf16[1,3,256,512]{3,2,1,0:T(8,128)(2,1)}, u32[]{:S(2)}) copy-start(bf16[1,3,256,512]{3,2,1,0:T(8,128)(2,1)} %get-tuple-element.12) | copy-start | bytes 2359300

commit v4 on v3

--- a/solution.py
+++ b/solution.py
@@ -11,7 +11,7 @@
 F32 = jnp.float32
 BF16 = jnp.bfloat16
 CHUNKS = 8
-AHEAD = 3
+AHEAD = 6
 HALVES = 2
 CONTRACT_LAST = (((1,), (1,)), ((), ()))
 CONTRACT_FIRST = (((0,), (0,)), ((), ()))
@@ -26,7 +26,7 @@
     rows_ref, cols_ref, ids_ref, count_ref, acts_hbm, top_hbm, w1_hbm, w2_hbm, table_hbm,
     grads_ref, first_ref, second_ref,
     acts_ref, top_ref, w1_ref, w2_ref, table_ref, load_sem,
-    adj_own, adj_out, adj_par, g_own, g_par, g_out, to_line, from_line, act_s, slope_s, dm_s, dpre_s, acc1, acc2,
+    adj_own, adj_out, adj_par, g_own, g_par, g_out, to_line, from_line, local_s, act_s, slope_s, dm_s, dpre_s, acc1, acc2,
     send_x1, send_x2, recv_x1, recv_x2, send_z1, send_z2, recv_z1, recv_z2,
     adj_ssem, adj_rsem, pass_ssem, own_ssem, own_rsem, par_ssem, par_rsem, term_ssem, term_rsem,
     x_ssem, x_rsem, z_ssem, z_rsem, az_ssem, az_rsem, ax_ssem, ax_rsem,
@@ -163,6 +163,45 @@
     greeted = 4 + has_below.astype(jnp.int32) + below_top.astype(jnp.int32)
     pl.semaphore_wait(barrier, greeted)
 
+    def spread(c):
+        @pl.when(below_top)
+        def _():
+            for f in range(halves):
+                own_copy(c, f).wait_recv()
+                pl.when(odd)(lambda: relay_copy(c, f).start())
+
+        for f in range(halves):
+            local_s[c, f] = dot(adj_own[c], g_own[c, f])
+        adj_copy(c).wait_recv()
+        pl.when(odd)(lambda: pass_copy(c).start())
+        for f in range(halves):
+            par_copy(c, f).wait_recv()
+            to_line[c, f] = dot(adj_par[c, rows:], g_par[c, f]).astype(BF16)
+            line_copy(c, f).start()
+        for f in range(halves):
+            local_s[c, f] += dot(adj_par[c, :rows], g_par[c, f])
+
+    def mlp(c):
+        for f in range(halves):
+            line_copy(c, f).wait_recv()
+            dm_s[c, :, f * width:(f + 1) * width] = (local_s[c, f] + from_line[c, f].astype(F32)).astype(BF16)
+        step = hidden // 4
+        for j in range(4):
+            at = slice(j * step, (j + 1) * step)
+            dact = dot(dm_s[c], w2_ref[0, at, :], CONTRACT_LAST)
+            dpre_s[c, :, at] = (dact * slope_s[c, :, at]).astype(BF16)
+        for f in range(halves):
+            at = slice(f * width, (f + 1) * width)
+            back = dot(dpre_s[c], w1_ref[0, at, :], CONTRACT_LAST)
+            g_out[c, f] = (g_own[c, f].astype(F32) + back).astype(BF16)
+
+            @pl.when(has_below)
+            def _():
+                own_copy(c, f).start()
+                pl.when(odd)(lambda: par_copy(c, f).start())
+
+            grads_ref[0, c, :, at] = g_out[c, f]
+
     @pl.when(top_sec)
     def _():
         load(4, top_hbm, top_ref).wait()
@@ -173,56 +212,36 @@
     load_acts.wait()
     load_w1.wait()
     load_w2.wait()
+    forward(0)
 
     @pl.when(below_top)
     def _():
         for c in range(1, groups):
             build(c)
-        for c in range(groups):
+        for c in range(1, groups):
             forward(c)
 
+    def prepare(c):
+        @pl.when(top_sec)
+        def _():
+            take_top(c)
+            build(c)
+            forward(c)
+
+    if groups > 1:
+        prepare(1)
+    spread(0)
     for c in range(groups):
-        @pl.when(below_top)
-        def _():
-            for f in range(halves):
-                own_copy(c, f).wait_recv()
-                pl.when(odd)(lambda: relay_copy(c, f).start())
-
-        local = [dot(adj_own[c], g_own[c, f]) for f in range(halves)]
-        adj_copy(c).wait_recv()
-        pl.when(odd)(lambda: pass_copy(c).start())
-        for f in range(halves):
-            par_copy(c, f).wait_recv()
-            to_line[c, f] = dot(adj_par[c, rows:], g_par[c, f]).astype(BF16)
-            line_copy(c, f).start()
-            local[f] = local[f] + dot(adj_par[c, :rows], g_par[c, f])
-
-        @pl.when(top_sec)
-        def _():
-            if c + 1 < groups:
-                take_top(c + 1)
-                build(c + 1)
-            forward(c)
-
-        if c > 0:
-            weight_grads(c - 1)
-        for f in range(halves):
-            line_copy(c, f).wait_recv()
-            dm_s[c, :, f * width:(f + 1) * width] = (local[f] + from_line[c, f].astype(F32)).astype(BF16)
-        step = hidden // 4
-        for j in range(4):
-            at = slice(j * step, (j + 1) * step)
-            dact = dot(dm_s[c], w2_ref[0, at, :], CONTRACT_LAST)
-            dpre_s[c, :, at] = (dact * slope_s[c, :, at]).astype(BF16)
-        for f in range(halves):
-            at = slice(f * width, (f + 1) * width)
-            back = dot(dpre_s[c], w1_ref[0, at, :], CONTRACT_LAST)
-            g_out[c, f] = (g_own[c, f].astype(F32) + back).astype(BF16)
-            pl.when(has_below)(lambda: own_copy(c, f).start())
-            pl.when(odd)(lambda: par_copy(c, f).start())
-            grads_ref[0, c, :, at] = g_out[c, f]
-
-    weight_grads(groups - 1)
+        if c + 2 < groups:
+            prepare(c + 2)
+        if c + 1 < groups:
+            spread(c + 1)
+        mlp(c)
+        if c + 2 < groups:
+            weight_grads(c)
+    for c in range(max(groups - 2, 0), groups):
+        weight_grads(c)
+
     half1 = feat // 2
     half2 = hidden // 2
     step1 = half1 // CHUNKS
@@ -366,6 +385,7 @@
             pltpu.VMEM((groups, rows, rows), BF16),
             *[pltpu.VMEM((groups, 2 * rows, rows), BF16)] * 2,
             *[half] * 5,
+            pltpu.VMEM((groups, HALVES, rows, width), F32),
             wide(BF16, hidden),
             wide(F32, hidden),
             wide(BF16, feat),

time: 140 us -> 130 us (0.929)
  Pallas kernels: 132 us -> 122 us
    pallas_call x1, Pallas kernels: 132 us -> 122 us  [shards(): pl.pallas_call(functools.partial(kernel, sections, nodes), out_shape=(jax...]
where the time goes in v4:
time: 130 us; the launch traced here: 129 us
  Pallas kernels  122 us (94%)
  other arithmetic  4.49 us (3%)
  local copies, waits for them, and re-layouts  2.2 us (2%)
    pallas_call x1, Pallas kernels, shards(): pl.pallas_call(functools.partial(kernel, sections, nodes), out_shape=(jax...  122 us
    broadcast_in_dim x2, other arithmetic, shards(): return (grads, first.astype(F32)[None], second.astype(F32)[None])  4.49 us

profile of v4, /device:TPU:0, one launch (start us, length us, event | category | flops | bytes accessed | tf_op | source)
XLA Modules:
  0.0 129.4 jit_solution(7016268513814861017)
XLA Ops:
  0.6 1.3 %copy.12.count_ref = s32[3,1]{1,0:T(4,128)} copy(s32[3,1]{0,1:T(1,128)} %param.17) | data formatting | bytes 24 | tf_op args[8]
  1.9 122.1 %relay_back.1 = (bf16[1,3,256,512]{3,2,1,0:T(8,128)(2,1)}, bf16[512,1024]{1,0:T(8,128)(2,1)}, bf16[1024,512]{1,0:T(8,128)(2,1)}) custom-call(s32[3,8]{1,0:T(4,128)} %rows_ref.1, s32[3,8]{1,0:T(4,128)} %cols_ref.1, s32[3,8]{1,0:T(4,128)} %ids_ref.1, s32[3,1]{1,0:T(4,128)} %copy.12.count_ref, bf16[1,3,256,512]{3,2,1,0:T(8,128)(2,1)} %acts_hbm.1, ...), custom_call_target="tpu_custom_call" | custom-call | tf_op jit(solution)/shard_map/relay_back/pallas_call | solution.py:373
  124.0 0.0 copy-start
  124.1 2.9 %bitcast_convert_fusion.1 = f32[1,512,1024]{2,1,0:T(8,128)} fusion(bf16[512,1024]{1,0:T(8,128)(2,1)} %get-tuple-element.7), kind=kLoop, calls=%fused_computation.1 | loop fusion | flops 524288 | bytes 3145728 | tf_op jit(solution)/shard_map/broadcast_in_dim | solution.py:407
  126.9 0.0 copy-done
  126.9 0.0 copy-start.1
  126.9 1.6 %bitcast_convert_fusion = f32[1,1024,512]{2,1,0:T(8,128)} fusion(bf16[1024,512]{1,0:T(8,128)(2,1)S(1)} %copy-done), kind=kLoop, calls=%fused_computation | loop fusion | flops 524288 | bytes 3145728 | tf_op jit(solution)/shard_map/broadcast_in_dim | solution.py:407
  128.5 0.0 copy-done.1
  128.5 0.9 copy.14
Async XLA Ops:
  124.0 2.9 %copy-start = (bf16[1024,512]{1,0:T(8,128)(2,1)S(1)}, bf16[1024,512]{1,0:T(8,128)(2,1)}, u32[]{:S(2)}) copy-start(bf16[1024,512]{1,0:T(8,128)(2,1)} %get-tuple-element.8) | copy-start | bytes 3145732
  126.9 1.6 %copy-start.1 = (bf16[1,3,256,512]{3,2,1,0:T(8,128)(2,1)S(1)}, bf16[1,3,256,512]{3,2,1,0:T(8,128)(2,1)}, u32[]{:S(2)}) copy-start(bf16[1,3,256,512]{3,2,1,0:T(8,128)(2,1)} %get-tuple-element.12) | copy-start | bytes 2359300

commit v5 on v4

--- a/solution.py
+++ b/solution.py
@@ -10,8 +10,9 @@
 MESH = pl.DeviceIdType.MESH
 F32 = jnp.float32
 BF16 = jnp.bfloat16
-CHUNKS = 8
-AHEAD = 6
+PAIRED = 4
+CHUNKS = 12
+LAG = 3
 HALVES = 2
 CONTRACT_LAST = (((1,), (1,)), ((), ()))
 CONTRACT_FIRST = (((0,), (0,)), ((), ()))
@@ -242,20 +243,19 @@
     for c in range(max(groups - 2, 0), groups):
         weight_grads(c)
 
-    half1 = feat // 2
-    half2 = hidden // 2
-    step1 = half1 // CHUNKS
-    step2 = half2 // CHUNKS
+    step1, step2 = recv_x1.shape[1], recv_x2.shape[1]
+
+    def place(kind, j, which):
+        step = (step1, step2)[kind]
+        if j < PAIRED:
+            return pl.ds(pl.multiple_of((which * PAIRED + j) * step, step), step)
+        return pl.ds((PAIRED + j) * step, step)
 
     def own(kind, j):
-        if kind == 0:
-            return pl.ds(pl.multiple_of(side * half1 + j * step1, step1), step1)
-        return pl.ds(pl.multiple_of(side * half2 + j * step2, step2), step2)
+        return place(kind, j, side)
 
     def other(kind, j):
-        if kind == 0:
-            return pl.ds(pl.multiple_of((1 - side) * half1 + j * step1, step1), step1)
-        return pl.ds(pl.multiple_of((1 - side) * half2 + j * step2, step2), step2)
+        return place(kind, j, 1 - side)
 
     acc = (acc1, acc2)
     outs = (first_ref, second_ref)
@@ -267,8 +267,9 @@
     has_away = (has_down, has_up)
 
     def x_copy(kind, j):
-        return remote(
-            send_x[kind].at[j], recv_x[kind].at[j], x_ssem.at[kind, j], x_rsem.at[kind, j], partner)
+        source = send_x if j < PAIRED else send_z
+        return remote(
+            source[kind].at[j], recv_x[kind].at[j], x_ssem.at[kind, j], x_rsem.at[kind, j], partner)
 
     def z_copy(kind, j):
         return remote(
@@ -287,7 +288,10 @@
         x_copy(kind, j).start()
 
     def reduce_chunk(kind, j):
-        value = acc[kind][own(kind, j), :] + recv_x[kind][j].astype(F32)
+        value = acc[kind][own(kind, j), :]
+        if j < PAIRED:
+            x_copy(kind, j).wait_recv()
+            value = value + recv_x[kind][j].astype(F32)
         send_z[kind][j] = value.astype(BF16)
 
         @pl.when(has_away[kind])
@@ -301,30 +305,45 @@
 
         @pl.when(jnp.logical_not(has_towards[kind]))
         def _():
-            outs[kind][own(kind, j), :] = send_z[kind][j]
-            az_copy(kind, j).start()
-            ax_copy(kind, j).start()
+            if j < PAIRED:
+                outs[kind][own(kind, j), :] = send_z[kind][j]
+                az_copy(kind, j).start()
+                ax_copy(kind, j).start()
+            else:
+                x_copy(kind, j).start()
 
     def gather_chunk(kind, j):
         @pl.when(has_towards[kind])
         def _():
             az_copy(kind, j).wait_recv()
             pl.when(has_away[kind])(lambda: az_copy(kind, j).start())
-            ax_copy(kind, j).start()
+            if j < PAIRED:
+                ax_copy(kind, j).start()
+
+    def finish_chunk(kind, j):
+        @pl.when(jnp.logical_not(has_towards[kind]))
+        def _():
+            x_copy(kind, j).wait_recv()
+            total = send_z[kind][j].astype(F32) + recv_x[kind][j].astype(F32)
+            outs[kind][own(kind, j), :] = total.astype(BF16)
+            az_copy(kind, j).start()
+
+    chunks = [*range(PAIRED, CHUNKS), *range(PAIRED)]
 
     def reduce_all(first):
-        order = [(kind, j) for kind in (first, 1 - first) for j in range(CHUNKS)]
-        for kind, j in order[:AHEAD]:
-            send_across(kind, j)
-        for i, (kind, j) in enumerate(order):
-            x_copy(kind, j).wait_recv()
-            if i + AHEAD < len(order):
-                send_across(*order[i + AHEAD])
-            reduce_chunk(kind, j)
+        order = [(kind, j) for kind in (first, 1 - first) for j in chunks]
+        for kind, j in order:
+            if j < PAIRED:
+                send_across(kind, j)
+        for i in range(len(order) + LAG):
+            if i < len(order):
+                reduce_chunk(*order[i])
+            if i >= LAG and order[i - LAG][1] >= PAIRED:
+                finish_chunk(*order[i - LAG])
 
     def gather_all(first):
         for kind in (first, 1 - first):
-            for j in range(CHUNKS):
+            for j in chunks:
                 gather_chunk(kind, j)
 
     early = along < line // 2
@@ -336,8 +355,11 @@
 
     for kind in range(2):
         for j in range(CHUNKS):
-            ax_copy(kind, j).wait()
-            x_copy(kind, j).wait_send()
+            if j < PAIRED:
+                ax_copy(kind, j).wait()
+                x_copy(kind, j).wait_send()
+            else:
+                pl.when(jnp.logical_not(has_towards[kind]))(lambda: x_copy(kind, j).wait_send())
             pl.when(has_towards[kind])(lambda: z_copy(kind, j).wait_send())
             pl.when(has_away[kind])(lambda: az_copy(kind, j).wait_send())
     for c in range(groups):
@@ -367,8 +389,8 @@
     width = feat // HALVES
     half = pltpu.VMEM((groups, HALVES, rows, width), BF16)
     wide = lambda kind, count: pltpu.VMEM((groups, rows, count), kind)
-    part1 = pltpu.VMEM((CHUNKS, feat // 2 // CHUNKS, hidden), BF16)
-    part2 = pltpu.VMEM((CHUNKS, hidden // 2 // CHUNKS, feat), BF16)
+    part1 = pltpu.VMEM((CHUNKS, feat // (CHUNKS + PAIRED), hidden), BF16)
+    part2 = pltpu.VMEM((CHUNKS, hidden // (CHUNKS + PAIRED), feat), BF16)
     dma = pltpu.SemaphoreType.DMA
     grads, first, second = pl.pallas_call(
         functools.partial(kernel, sections, nodes),

time: 130 us -> 134 us (1.031)
  Pallas kernels: 122 us -> 126 us
    pallas_call x1, Pallas kernels: 122 us -> 126 us  [shards(): pl.pallas_call(functools.partial(kernel, sections, nodes), out_shape=(jax...]
where the time goes in v5:
time: 134 us
  Pallas kernels  126 us (94%)
  other arithmetic  4.49 us (3%)
  local copies, waits for them, and re-layouts  2.2 us (2%)
    pallas_call x1, Pallas kernels, shards(): pl.pallas_call(functools.partial(kernel, sections, nodes), out_shape=(jax...  126 us
    broadcast_in_dim x2, other arithmetic, shards(): return (grads, first.astype(F32)[None], second.astype(F32)[None])  4.49 us

profile of v5, /device:TPU:0, one launch (start us, length us, event | category | flops | bytes accessed | tf_op | source)
XLA Modules:
  0.0 133.8 jit_solution(15631250866178167746)
XLA Ops:
  0.6 1.3 copy.12.count_ref
  1.9 126.4 %relay_back.1 = (bf16[1,3,256,512]{3,2,1,0:T(8,128)(2,1)}, bf16[512,1024]{1,0:T(8,128)(2,1)}, bf16[1024,512]{1,0:T(8,128)(2,1)}) custom-call(s32[3,8]{1,0:T(4,128)} %rows_ref.1, s32[3,8]{1,0:T(4,128)} %cols_ref.1, s32[3,8]{1,0:T(4,128)} %ids_ref.1, s32[3,1]{1,0:T(4,128)} %copy.12.count_ref, bf16[1,3,256,512]{3,2,1,0:T(8,128)(2,1)} %acts_hbm.1, ...), custom_call_target="tpu_custom_call" | custom-call | tf_op jit(solution)/shard_map/relay_back/pallas_call | solution.py:395
  128.4 0.0 copy-start
  128.4 2.9 %bitcast_convert_fusion.1 = f32[1,512,1024]{2,1,0:T(8,128)} fusion(bf16[512,1024]{1,0:T(8,128)(2,1)} %get-tuple-element.7), kind=kLoop, calls=%fused_computation.1 | loop fusion | flops 524288 | bytes 3145728 | tf_op jit(solution)/shard_map/broadcast_in_dim | solution.py:429
  131.3 0.0 copy-done
  131.3 0.0 copy-start.1
  131.3 1.6 %bitcast_convert_fusion = f32[1,1024,512]{2,1,0:T(8,128)} fusion(bf16[1024,512]{1,0:T(8,128)(2,1)S(1)} %copy-done), kind=kLoop, calls=%fused_computation | loop fusion | flops 524288 | bytes 3145728 | tf_op jit(solution)/shard_map/broadcast_in_dim | solution.py:429
  132.9 0.0 copy-done.1
  132.9 0.9 copy.14
Async XLA Ops:
  128.4 2.9 %copy-start = (bf16[1024,512]{1,0:T(8,128)(2,1)S(1)}, bf16[1024,512]{1,0:T(8,128)(2,1)}, u32[]{:S(2)}) copy-start(bf16[1024,512]{1,0:T(8,128)(2,1)} %get-tuple-element.8) | copy-start | bytes 3145732
  131.3 1.6 %copy-start.1 = (bf16[1,3,256,512]{3,2,1,0:T(8,128)(2,1)S(1)}, bf16[1,3,256,512]{3,2,1,0:T(8,128)(2,1)}, u32[]{:S(2)}) copy-start(bf16[1,3,256,512]{3,2,1,0:T(8,128)(2,1)} %get-tuple-element.12) | copy-start | bytes 2359300
